TPU v7x, 32 devices: a whole 2x2x4 slice. The times are simulated.
32 devices in a mesh: group: 2 (over y), train: 4 (over z), module: 4 (over x, core).
Axes of the slice: x: 2, y: 2, z: 4, core: 2. Of those that a mesh axis runs over, the one named last changes fastest.
Arguments:
- query_tokens: int32 [128, 8], P(('group', 'train')), parts along dimension 0, may hold values from 0 to 152063, as said below
- activations: bfloat16 [4, 128, 8, 5120], P('module', ('group', 'train')), parts along dimension 1, may hold values from -6 to 6
- out_grads: bfloat16 [4, 128, 8, 5120], P('module', ('group', 'train')), parts along dimension 1, may hold values from -6 to 6
- in_proj: bfloat16 [4, 5120, 64], P('module'), may hold values from -0.078125 to 0.078125
- out_proj: bfloat16 [4, 5120, 64], P('module'), may hold values from -0.078125 to 0.078125
- in_factor: float32 [4, 64, 64], P('module')
- out_factor: float32 [4, 64, 64], P('module')
- train_store: bfloat16 [4, 2048, 4096], P('module', ('group', 'train')), parts along dimension 1, may hold values from -0.375 to 0.375
- store_rows: int32 [4, 8], P('module', ('group', 'train')), parts along dimension 1, may hold values from 64 to 256, as said below
Outputs:
- scores: float32 [128, 1024], P('group', ('train', 'module')), parts along dimension 0
There are 2 independent parts, one for each index of `group`. A program takes and returns all parts, laid end to end along the dimension named above; an argument that names none is the same for every part. Nothing has to cross between parts.
Inputs may be any that keep to these rules, and one draw needn't show every extreme that they name: `query_tokens`: 0 marks padding, which fills a tail of each query; each query has at least 4 and fewer than 8 real tokens. `store_rows`: rows of a store shard at or past its count hold stale data.
All inputs are finite; a program needn't handle non-finite values.
Results may differ from a plain program's by a relative error of at most 0.0029.
Values may be sent and summed in bfloat16 or wider, within the bound.
A program may use at most 64 MiB of HBM per device.

v0:
```python
import jax
import jax.numpy as jnp
from jax import lax
from jax.sharding import PartitionSpec as P


def on_device(
    query_tokens,
    activations,
    out_grads,
    in_proj,
    out_proj,
    in_factor,
    out_factor,
    train_store,
    store_rows,
):
    local_queries = activations.shape[1]
    slots = activations.shape[2]
    width = activations.shape[3]
    rank = in_proj.shape[2]
    store_local = train_store[0]
    store_count = store_local.shape[0]
    valid = (jnp.arange(store_count, dtype=jnp.int32) < store_rows[0, 0]).astype(jnp.float32)
    keep = (query_tokens > 0).astype(jnp.float32)
    counted = jnp.sum(keep, axis=1)
    acts = activations[0, 0 : 0 + local_queries].reshape(local_queries * slots, width)
    grads = out_grads[0, 0 : 0 + local_queries].reshape(local_queries * slots, width)
    xin = jnp.dot(acts, in_proj[0], preferred_element_type=jnp.float32).reshape(
        local_queries, slots, rank
    )
    gout = jnp.dot(grads, out_proj[0], preferred_element_type=jnp.float32).reshape(
        local_queries, slots, rank
    )
    gout = gout * keep[:, :, None]
    grad = (
        jnp.einsum("qto,qti->qoi", gout, xin, precision=lax.Precision.HIGHEST)
        / counted[:, None, None]
    )
    left = jnp.einsum("ab,qbi->qai", out_factor[0], grad, precision=lax.Precision.HIGHEST)
    both = jnp.einsum("qai,ic->qac", left, in_factor[0], precision=lax.Precision.HIGHEST)
    prepared = both.reshape(local_queries, rank * rank).astype(jnp.bfloat16)
    product = jnp.einsum(
        "qk,tk->qt",
        lax.all_gather(prepared, "train", axis=0, tiled=True),
        store_local,
        preferred_element_type=jnp.float32,
    )
    partial_value = product * valid[None, :]
    summed = lax.psum(partial_value, "module")
    share = store_count // lax.axis_size("module")
    return lax.dynamic_slice_in_dim(summed, lax.axis_index("module") * share, share, 1)


def solution(mesh):
    placed = (
        P(("group", "train"), None),
        P("module", ("group", "train"), None, None),
        P("module", ("group", "train"), None, None),
        P("module", None, None),
        P("module", None, None),
        P("module", None, None),
        P("module", None, None),
        P("module", ("group", "train"), None),
        P("module", ("group", "train")),
    )
    return jax.shard_map(
        on_device,
        mesh=mesh,
        in_specs=placed,
        out_specs=P("group", ("train", "module")),
        check_vma=False,
    )
```

profile of v0, /device:TPU:0, one launch (start us, length us, event | category | flops | bytes accessed | tf_op | source)
XLA Modules:
  0.0 74.1 jit_solution(4679856034632086396)
XLA Ops:
  6.5 0.0 copy-start
  6.5 0.0 copy-start.1
  6.5 0.0 all-reduce.2.cloned.1.call-start
  6.5 0.8 %compare_convert_fusion = f32[16,8]{0,1:T(8,128)S(1)} fusion(s32[16,8]{0,1:T(8,128)} %param.9), kind=kLoop, calls=%fused_computation.15 | loop fusion | flops 256 | bytes 1024 | tf_op jit(solution)/shard_map/convert_element_type | solution.py:25
  7.4 0.8 %fusion.16 = f32[16]{0:T(128)S(1)} fusion(s32[16,8]{0,1:T(8,128)} %param.9), kind=kLoop, calls=%fused_computation.18 | loop fusion | flops 368 | bytes 576 | tf_op jit(solution)/shard_map/reduce_sum | solution.py:26
  8.2 0.1 copy.10
  8.2 0.0 copy-start.2
  8.2 2.0 %fusion.2 = f32[16,8,64]{2,1,0:T(8,128)S(1)} fusion(bf16[1,16,8,5120]{3,2,1,0:T(8,128)(2,1)} %param.10, bf16[1,5120,64]{1,2,0:T(8,128)(2,1)} %param.12), kind=kOutput, calls=%fused_computation.2 | convolution fusion | flops 83886080 | bytes 1998848 | tf_op jit(solution)/shard_map/dot_general | solution.py:29
  10.3 0.0 copy-done.1
  10.3 0.0 copy-done.2
  10.3 0.5 fusion.6
  10.8 0.0 copy-start.3
  10.8 0.0 copy-start.4
  10.8 1.0 %convolution_divide_fusion = f32[16,64,64]{2,1,0:T(8,128)S(1)} fusion(f32[16,8,64]{2,1,0:T(8,128)S(1)} %fusion.6, f32[16,8,64]{2,1,0:T(8,128)S(1)} %fusion.2, f32[16]{0:T(128)S(1)} %fusion.16), kind=kOutput, calls=%fused_computation.7 | convolution fusion | flops 6356992 | bytes 327744 | tf_op jit(solution)/shard_map/qto,qti->qoi/dot_general | solution.py:37
  11.8 0.0 copy-done.3
  11.9 0.6 convolution_bitcast_fusion
  12.5 0.0 copy-done.4
  12.5 0.6 convolution_convert_fusion
  13.0 0.3 convert_element_type.18
  13.3 17.4 %all_gather.3 = bf16[64,4096]{1,0:T(8,128)(2,1)S(1)} all-gather(bf16[16,4096]{1,0:T(8,128)(2,1)S(1)} %convert_element_type.18), channel_id=1, replica_groups=mesh['group'=2,'train'=4,'module'=4] {'train'}, dimensions={0}, use_global_device_ids=true | all-gather | bytes 655360 | tf_op jit(solution)/shard_map/all_gather | solution.py:45
  31.3 0.0 copy-done
  31.4 1.4 %fusion.9 = f32[64,256]{1,0:T(8,128)} fusion(bf16[64,4096]{1,0:T(8,128)(2,1)S(1)} %all_gather.3, bf16[1,256,4096]{2,1,0:T(8,128)(2,1)S(1)} %copy-done, f32[256]{0:T(256)S(1)} %compare_convert_fusion.1), kind=kOutput, calls=%fused_computation.10 | convolution fusion | flops 134234112 | bytes 2688000 | tf_op jit(solution)/shard_map/qk,tk->qt/dot_general | solution.py:43
  32.7 0.0 all-reduce.2.cloned.1.call-update
  32.8 33.0 %all-reduce.2.cloned.1.call-done = f32[64,256]{1,0:T(8,128)} async-done(((f32[64,256]{1,0:T(8,128)}), f32[64,256]{1,0:T(8,128)}) %all-reduce.2.cloned.1.call-update) | async-done | bytes 65552 | tf_op jit(solution)/shard_map/psum | solution.py:50
  65.8 1.4 %constant_dynamic-slice_fusion = f32[64,64]{1,0:T(8,128)} fusion(f32[64,256]{1,0:T(8,128)} %all-reduce.2.cloned.1.call-done, s32[]{:T(128)S(6)} %select_n.3), kind=kLoop, calls=%fused_computation.17 | loop fusion | bytes 32772 | tf_op jit(solution)/shard_map/dynamic_slice | solution.py:52
  (1 shorter events, 0.0 us)
Async XLA Ops:
  6.5 24.8 %copy-start = (bf16[1,256,4096]{2,1,0:T(8,128)(2,1)S(1)}, bf16[1,256,4096]{2,1,0:T(8,128)(2,1)}, u32[]{:S(2)}) copy-start(bf16[1,256,4096]{2,1,0:T(8,128)(2,1)} %param.16) | copy-start | bytes 6291460
  6.5 3.7 %copy-start.1 = (bf16[1,16,8,5120]{3,2,1,0:T(8,128)(2,1)S(1)}, bf16[1,16,8,5120]{3,2,1,0:T(8,128)(2,1)}, u32[]{:S(2)}) copy-start(bf16[1,16,8,5120]{3,2,1,0:T(8,128)(2,1)} %param.11) | copy-start | bytes 3932164
  6.5 59.2 %all-reduce.2.cloned.1.call-start = ((), (), s32[]{:S(2)}) async-start(), calls=%async_computation | async-start | bytes 131072 | tf_op jit(solution)/shard_map/psum | solution.py:50
  8.2 2.1 %copy-start.2 = (bf16[1,5120,64]{1,2,0:T(8,128)(2,1)S(1)}, bf16[1,5120,64]{1,2,0:T(8,128)(2,1)}, u32[]{:S(2)}) copy-start(bf16[1,5120,64]{1,2,0:T(8,128)(2,1)} %param.13) | copy-start | bytes 1966084
  10.8 1.0 %copy-start.3 = (f32[1,64,64]{2,1,0:T(8,128)S(1)}, f32[1,64,64]{2,1,0:T(8,128)}, u32[]{:S(2)}) copy-start(f32[1,64,64]{2,1,0:T(8,128)} %param.15) | copy-start | bytes 49156
  10.8 1.7 %copy-start.4 = (f32[1,64,64]{2,1,0:T(8,128)S(1)}, f32[1,64,64]{2,1,0:T(8,128)}, u32[]{:S(2)}) copy-start(f32[1,64,64]{2,1,0:T(8,128)} %param.14) | copy-start | bytes 49156
Sparse Core Ops, SparseCore 0:
  32.9 32.8 all-reduce.1
where the time goes:
time: 74.3 us; the launch traced here: 74.1 us
  waiting for transfers between devices  33 us (44%)
  blocking collectives  17.4 us (23%)
  between operations  14.2 us (19%)
  matrix products  6.11 us (8%)
  local copies, waits for them, and re-layouts  1.81 us (2%)
  other arithmetic  1.62 us (2%)
    psum x1, waiting for transfers between devices, on_device(): summed = lax.psum(partial_value, 'module')  33 us
    all_gather x1, blocking collectives, on_device(): lax.all_gather(prepared, 'train', axis=0, tiled=True)  17.4 us
    dot_general x1, matrix products, on_device(): jnp.dot(acts, in_proj[0], preferred_element_type=jnp.float32)  2.04 us
  transfers between devices with their start and end apart: 1, of which 1 were waited for; matrix products, arithmetic and copies ran while one was open for 0% of the time, Pallas kernels for 0%

commit v1 on v0

v1 whole, which is shorter than its diff:
```python
import functools
import math

import jax
import jax.numpy as jnp
from jax import lax
from jax.experimental import pallas as pl
from jax.experimental.pallas import tpu as pltpu
from jax.sharding import PartitionSpec as P

MESH = pl.DeviceIdType.MESH
HIGH = lax.Precision.HIGHEST
NT = (((1,), (1,)), ((), ()))
CHUNKS = 4


def onehot(condition):
    return jnp.where(condition, 1.0, 0.0).astype(jnp.bfloat16)


def kernel(
    n,
    m,
    tok_hbm,
    acts_hbm,
    grads_hbm,
    inp_hbm,
    outp_hbm,
    inf_hbm,
    outf_hbm,
    store_hbm,
    rows,
    out_ref,
    tok,
    acts,
    grads,
    inp,
    outp,
    inf,
    outf,
    store,
    spread,
    uv,
    held,
    pre,
    part,
    parts_in,
    load_sem,
    small_sem,
    send_sem,
    recv_sem,
    psend_sem,
    precv_sem,
):
    slots, queries = tok.shape
    used = slots - 1
    rank, width = inp.shape
    wide = rank * rank
    share = out_ref.shape[1]
    group = part.shape[3] // queries
    me = lax.axis_index("train")
    mod = lax.axis_index("module")
    step = width // CHUNKS

    loads = []
    for c in range(CHUNKS):
        at = pl.ds(c * step, step)
        row = []
        for i, (src, dst) in enumerate(
            ((grads_hbm, grads), (outp_hbm, outp), (acts_hbm, acts), (inp_hbm, inp))
        ):
            copy = pltpu.make_async_copy(src.at[:, at], dst.at[:, at], load_sem.at[c, i])
            copy.start()
            row.append(copy)
        loads.append(row)
    smalls = []
    for i, (src, dst) in enumerate(
        ((tok_hbm, tok), (outf_hbm, outf), (inf_hbm, inf), (store_hbm, store))
    ):
        copy = pltpu.make_async_copy(src, dst, small_sem.at[i])
        copy.start()
        smalls.append(copy)

    barrier = pltpu.get_barrier_semaphore()

    def greet(k, carry):
        pl.semaphore_signal(
            barrier, inc=1, device_id={"train": lax.rem(me + k, n)}, device_id_type=MESH
        )
        return carry

    lax.fori_loop(1, n, greet, 0, unroll=n <= 4)
    for k in range(1, m):
        pl.semaphore_signal(
            barrier, inc=1, device_id={"module": lax.rem(mod + k, m)}, device_id_type=MESH
        )

    k_at = lax.broadcasted_iota(jnp.int32, (4 * rank, wide), 0) % (2 * rank)
    n_at = lax.broadcasted_iota(jnp.int32, (4 * rank, wide), 1) // rank
    spread[:, 0:wide] = onehot(k_at == n_at)
    k_at = lax.broadcasted_iota(jnp.int32, (4 * rank, 2 * rank), 0) % (2 * rank)
    n_at = lax.broadcasted_iota(jnp.int32, (4 * rank, 2 * rank), 1) % rank
    spread[:, wide : wide + 2 * rank] = onehot(k_at == n_at + rank)

    smalls[0].wait()
    keep = onehot(tok[...] > 0)
    r_at = lax.broadcasted_iota(jnp.int32, (slots * queries, queries), 0)
    q_at = lax.broadcasted_iota(jnp.int32, (slots * queries, queries), 1)
    of_query = lax.dot_general(
        onehot(r_at % queries == q_at), keep, NT, preferred_element_type=jnp.float32
    )
    counted = jnp.sum(of_query, axis=1, keepdims=True)
    r_at = lax.broadcasted_iota(jnp.int32, (slots * queries, slots), 0)
    t_at = lax.broadcasted_iota(jnp.int32, (slots * queries, slots), 1)
    kept = jnp.sum(jnp.where(r_at // queries == t_at, of_query, 0.0), axis=1, keepdims=True)
    lane = lax.broadcasted_iota(jnp.int32, (slots * queries, 2 * rank), 1)
    weight = jnp.where(lane < rank, kept / counted, 1.0)

    gout = jnp.zeros((slots * queries, rank), jnp.float32)
    xin = jnp.zeros((slots * queries, rank), jnp.float32)
    for c in range(CHUNKS):
        at = slice(c * step, (c + 1) * step)
        loads[c][0].wait()
        loads[c][1].wait()
        gout += lax.dot_general(grads[:, at], outp[:, at], NT, preferred_element_type=jnp.float32)
        loads[c][2].wait()
        loads[c][3].wait()
        xin += lax.dot_general(acts[:, at], inp[:, at], NT, preferred_element_type=jnp.float32)

    smalls[1].wait()
    smalls[2].wait()
    uv[:, 0:rank] = lax.dot_general(
        gout, outf[...], NT, precision=HIGH, preferred_element_type=jnp.float32
    )
    uv[:, rank : 2 * rank] = jnp.dot(
        xin, inf[...], precision=HIGH, preferred_element_type=jnp.float32
    )
    for t in range(used):
        at = slice(t * queries, (t + 1) * queries)
        both = uv[pl.ds(t, queries, stride=slots), :] * weight[at]
        high = both.astype(jnp.bfloat16)
        low = (both - high.astype(jnp.float32)).astype(jnp.bfloat16)
        held[me, at, 0 : 2 * rank] = high
        held[me, at, 2 * rank : 4 * rank] = low

    pl.semaphore_wait(barrier, n - 1 + m - 1)

    def exchange(k):
        return pltpu.make_async_remote_copy(
            src_ref=held.at[me],
            dst_ref=held.at[me],
            send_sem=send_sem.at[k],
            recv_sem=recv_sem.at[k],
            device_id={"train": lax.rem(me + k, n)},
            device_id_type=MESH,
        )

    def send(k, carry):
        exchange(k).start()
        return carry

    lax.fori_loop(1, n, send, 0, unroll=n <= 4)

    def expand(s):
        block = held[s]
        v = jnp.dot(
            block, spread[:, wide : wide + 2 * rank], preferred_element_type=jnp.float32
        )
        v = jnp.concatenate([v, v], axis=1)
        for j in range(wide // (4 * rank)):
            at = slice(j * 4 * rank, (j + 1) * 4 * rank)
            u = jnp.dot(block, spread[:, at], preferred_element_type=jnp.float32)
            prod = u * v
            total = prod[0:queries]
            for t in range(1, used):
                total += prod[t * queries : (t + 1) * queries]
            pre[s // group, pl.ds(pl.multiple_of((s % group) * queries, queries), queries), at] = (
                total.astype(jnp.bfloat16)
            )

    expand(me)

    def arrive(k, carry):
        pltpu.make_async_copy(held.at[me], held.at[me], recv_sem.at[k]).wait()
        expand(lax.rem(me - k + n, n))
        return carry

    lax.fori_loop(1, n, arrive, 0)

    smalls[3].wait()
    r_at = lax.broadcasted_iota(jnp.int32, (store.shape[0], 1), 0)
    valid = r_at < rows[0, 0]

    def score(b, carry):
        product = lax.dot_general(store[...], pre[b], NT, preferred_element_type=jnp.float32)
        product = jnp.where(valid, product, 0.0)
        for j in range(m):
            part[j, b] = product[j * share : (j + 1) * share]
        return carry

    blocks = n // group
    lax.fori_loop(0, blocks, score, 0, unroll=blocks == 1)

    def reduce(k):
        to = lax.rem(mod + k, m)
        return pltpu.make_async_remote_copy(
            src_ref=part.at[to],
            dst_ref=parts_in.at[k],
            send_sem=psend_sem.at[k],
            recv_sem=precv_sem.at[k],
            device_id={"module": to},
            device_id_type=MESH,
        )

    for k in range(1, m):
        reduce(k).start()

    def sent(k, carry):
        exchange(k).wait_send()
        return carry

    lax.fori_loop(1, n, sent, 0, unroll=n <= 4)
    for k in range(1, m):
        reduce(k).wait_recv()

    def finish(b, carry):
        total = part[mod, b]
        for k in range(1, m):
            total += parts_in[k, b]
        size = group * queries
        out_ref[pl.ds(pl.multiple_of(b * size, size), size), :] = total.T
        return carry

    lax.fori_loop(0, blocks, finish, 0, unroll=blocks == 1)
    for k in range(1, m):
        reduce(k).wait_send()


def on_device(
    n,
    m,
    query_tokens,
    activations,
    out_grads,
    in_proj,
    out_proj,
    in_factor,
    out_factor,
    train_store,
    store_rows,
):
    queries, slots = query_tokens.shape
    width, rank = in_proj.shape[1:]
    count, wide = train_store.shape[1:]
    share = count // m
    group = math.gcd(n, 4)
    blocks = n // group
    bf16, f32, i32 = jnp.bfloat16, jnp.float32, jnp.int32
    scratch = [
        pltpu.VMEM((slots, queries), i32),
        pltpu.VMEM((queries * slots, width), bf16),
        pltpu.VMEM((queries * slots, width), bf16),
        pltpu.VMEM((rank, width), bf16),
        pltpu.VMEM((rank, width), bf16),
        pltpu.VMEM((rank, rank), f32),
        pltpu.VMEM((rank, rank), f32),
        pltpu.VMEM((count, wide), bf16),
        pltpu.VMEM((4 * rank, wide + 2 * rank), bf16),
        pltpu.VMEM((queries * slots, 2 * rank), f32),
        pltpu.VMEM((n, (slots - 1) * queries, 4 * rank), bf16),
        pltpu.VMEM((blocks, group * queries, wide), bf16),
        pltpu.VMEM((m, blocks, share, group * queries), f32),
        pltpu.VMEM((m, blocks, share, group * queries), f32),
        pltpu.SemaphoreType.DMA((CHUNKS, 4)),
        pltpu.SemaphoreType.DMA((4,)),
        pltpu.SemaphoreType.DMA((n,)),
        pltpu.SemaphoreType.DMA((n,)),
        pltpu.SemaphoreType.DMA((m,)),
        pltpu.SemaphoreType.DMA((m,)),
    ]
    return pl.pallas_call(
        functools.partial(kernel, n, m),
        out_shape=jax.ShapeDtypeStruct((n * queries, share), f32),
        in_specs=[pl.BlockSpec(memory_space=pl.ANY)] * 8 + [pl.BlockSpec(memory_space=pltpu.SMEM)],
        out_specs=pl.BlockSpec(memory_space=pltpu.VMEM),
        scratch_shapes=scratch,
        compiler_params=pltpu.CompilerParams(
            collective_id=0, has_side_effects=True, vmem_limit_bytes=56 * 1024 * 1024
        ),
    )(
        query_tokens.T,
        activations.reshape(queries * slots, width),
        out_grads.reshape(queries * slots, width),
        jnp.swapaxes(in_proj[0], 0, 1),
        jnp.swapaxes(out_proj[0], 0, 1),
        in_factor[0],
        out_factor[0],
        train_store[0],
        store_rows,
    )


def solution(mesh):
    placed = (
        P(("group", "train"), None),
        P("module", ("group", "train"), None, None),
        P("module", ("group", "train"), None, None),
        P("module", None, None),
        P("module", None, None),
        P("module", None, None),
        P("module", None, None),
        P("module", ("group", "train"), None),
        P("module", ("group", "train")),
    )
    return jax.shard_map(
        functools.partial(on_device, mesh.shape["train"], mesh.shape["module"]),
        mesh=mesh,
        in_specs=placed,
        out_specs=P("group", ("train", "module")),
        check_vma=False,
    )
```

time: 74.3 us -> 21.3 us (0.29)
  waiting for transfers between devices: 33 us -> 0 us
  Pallas kernels: 0 us -> 19.1 us
  blocking collectives: 17.4 us -> 0 us
  between operations: 14.2 us -> 0.66 us
  matrix products: 6.11 us -> 0 us
  other arithmetic: 1.62 us -> 0 us
    psum x1 -> x0, waiting for transfers between devices: 33 us -> none  [on_device(): summed = lax.psum(partial_value, 'module')]
    pallas_call x0 -> x1, Pallas kernels: none -> 19.1 us  [on_device(): pl.pallas_call(functools.partial(kernel, n, m), out_shape=jax.ShapeDtypeS...]
    all_gather x1 -> x0, blocking collectives: 17.4 us -> none  [on_device(): lax.all_gather(prepared, 'train', axis=0, tiled=True)]
    dot_general x6 -> x0, matrix products: 6.11 us -> none  [the longest x1 2.04 us: on_device(): jnp.dot(acts, in_proj[0], preferred_element_type=jnp.float32)]
    dynamic_slice x1 -> x0, local copies, waits for them, and re-layouts: 1.45 us -> none  [on_device(): lax.dynamic_slice_in_dim(summed, lax.axis_index('module') * share, share, 1)]
    unnamed x10 -> x1, local copies, waits for them, and re-layouts: 0.02 us -> 1.38 us
    convert_element_type x2 -> x0, other arithmetic: 0.85 us -> none  [the longest x1 0.84 us: on_device(): keep = (query_tokens > 0).astype(jnp.float32)]
    reduce_sum x1 -> x0, other arithmetic: 0.77 us -> none  [on_device(): counted = jnp.sum(keep, axis=1)]
  transfers between devices with their start and end apart: 1 -> 0, of which waited for: 1 -> 0; matrix products, arithmetic and copies ran while one was open for 0% -> 0% of each run, Pallas kernels for 0% -> 0%
where the time goes in v1:
time: 21.3 us; the launch traced here: 21.1 us
  Pallas kernels  19.1 us (90%)
  local copies, waits for them, and re-layouts  1.38 us (6%)
  between operations  0.66 us (3%)
    pallas_call x1, Pallas kernels, on_device(): pl.pallas_call(functools.partial(kernel, n, m), out_shape=jax.ShapeDtypeS...  19.1 us
    unnamed x1, local copies, waits for them, and re-layouts  1.38 us

profile of v1, /device:TPU:0, one launch (start us, length us, event | category | flops | bytes accessed | tf_op | source)
XLA Modules:
  0.0 21.1 jit_solution(6347796691552927)
XLA Ops:
  0.7 19.1 %shard_map.91 = f32[64,64]{1,0:T(8,128)} custom-call(s32[8,16]{1,0:T(8,128)} %bitcast.19, bf16[128,5120]{1,0:T(8,128)(2,1)} %bitcast.13, bf16[128,5120]{1,0:T(8,128)(2,1)} %bitcast.14, bf16[64,5120]{1,0:T(8,128)(2,1)} %bitcast.15, bf16[64,5120]{1,0:T(8,128)(2,1)} %bitcast.16, f32[64,64]{1,0:T(8,128)} %bitcast.17, f32[64,64]{1,0:T(8,128)} %bitcast.18, ...), custom_call_target="tpu_custom_call" | custom-call | tf_op jit(solution)/shard_map/pallas_call | solution.py:281
  19.7 1.4 %copy.12 = f32[64,64]{1,0:T(8,128)} copy(f32[64,64]{1,0:T(8,128)} %shard_map.91) | data formatting | bytes 32768

commit v2 on v1

--- a/solution.py
+++ b/solution.py
@@ -57,50 +57,56 @@
     rank, width = inp.shape
     wide = rank * rank
     share = out_ref.shape[1]
-    group = part.shape[3] // queries
+    group = part.shape[3] // (2 * queries)
     me = lax.axis_index("train")
     mod = lax.axis_index("module")
     step = width // CHUNKS
 
-    loads = []
-    for c in range(CHUNKS):
-        at = pl.ds(c * step, step)
-        row = []
-        for i, (src, dst) in enumerate(
-            ((grads_hbm, grads), (outp_hbm, outp), (acts_hbm, acts), (inp_hbm, inp))
-        ):
-            copy = pltpu.make_async_copy(src.at[:, at], dst.at[:, at], load_sem.at[c, i])
-            copy.start()
-            row.append(copy)
-        loads.append(row)
+    barrier = pltpu.get_barrier_semaphore()
+
+    def greet(k, carry):
+        pl.semaphore_signal(
+            barrier, inc=1, device_id={"train": lax.rem(me + k, n)}, device_id_type=MESH
+        )
+        return carry
+
+    lax.fori_loop(1, n, greet, 0, unroll=n <= 4)
+    for k in range(1, m):
+        pl.semaphore_signal(
+            barrier, inc=1, device_id={"module": lax.rem(mod + k, m)}, device_id_type=MESH
+        )
+
     smalls = []
     for i, (src, dst) in enumerate(
-        ((tok_hbm, tok), (outf_hbm, outf), (inf_hbm, inf), (store_hbm, store))
+        ((tok_hbm, tok), (outf_hbm, outf), (inf_hbm, inf))
     ):
         copy = pltpu.make_async_copy(src, dst, small_sem.at[i])
         copy.start()
         smalls.append(copy)
-
-    barrier = pltpu.get_barrier_semaphore()
-
-    def greet(k, carry):
-        pl.semaphore_signal(
-            barrier, inc=1, device_id={"train": lax.rem(me + k, n)}, device_id_type=MESH
-        )
-        return carry
-
-    lax.fori_loop(1, n, greet, 0, unroll=n <= 4)
-    for k in range(1, m):
-        pl.semaphore_signal(
-            barrier, inc=1, device_id={"module": lax.rem(mod + k, m)}, device_id_type=MESH
-        )
-
-    k_at = lax.broadcasted_iota(jnp.int32, (4 * rank, wide), 0) % (2 * rank)
-    n_at = lax.broadcasted_iota(jnp.int32, (4 * rank, wide), 1) // rank
+    loads = []
+    for i, pair in enumerate((((grads_hbm, grads), (outp_hbm, outp)), ((acts_hbm, acts), (inp_hbm, inp)))):
+        column = []
+        for c in range(CHUNKS):
+            at = pl.ds(c * step, step)
+            row = []
+            for h, (src, dst) in enumerate(pair):
+                copy = pltpu.make_async_copy(
+                    src.at[:, at], dst.at[:, at], load_sem.at[i, c, h]
+                )
+                copy.start()
+                row.append(copy)
+            column.append(row)
+        loads.append(column)
+    copy = pltpu.make_async_copy(store_hbm, store, small_sem.at[3])
+    copy.start()
+    smalls.append(copy)
+
+    k_at = lax.broadcasted_iota(jnp.int32, (2 * rank, wide), 0) % rank
+    n_at = lax.broadcasted_iota(jnp.int32, (2 * rank, wide), 1) // rank
     spread[:, 0:wide] = onehot(k_at == n_at)
-    k_at = lax.broadcasted_iota(jnp.int32, (4 * rank, 2 * rank), 0) % (2 * rank)
-    n_at = lax.broadcasted_iota(jnp.int32, (4 * rank, 2 * rank), 1) % rank
-    spread[:, wide : wide + 2 * rank] = onehot(k_at == n_at + rank)
+    k_at = lax.broadcasted_iota(jnp.int32, (2 * rank, 2 * rank), 0) % rank
+    n_at = lax.broadcasted_iota(jnp.int32, (2 * rank, 2 * rank), 1) % rank
+    spread[:, wide : wide + 2 * rank] = onehot(k_at == n_at)
 
     smalls[0].wait()
     keep = onehot(tok[...] > 0)
@@ -113,58 +119,55 @@
     r_at = lax.broadcasted_iota(jnp.int32, (slots * queries, slots), 0)
     t_at = lax.broadcasted_iota(jnp.int32, (slots * queries, slots), 1)
     kept = jnp.sum(jnp.where(r_at // queries == t_at, of_query, 0.0), axis=1, keepdims=True)
-    lane = lax.broadcasted_iota(jnp.int32, (slots * queries, 2 * rank), 1)
-    weight = jnp.where(lane < rank, kept / counted, 1.0)
-
-    gout = jnp.zeros((slots * queries, rank), jnp.float32)
-    xin = jnp.zeros((slots * queries, rank), jnp.float32)
-    for c in range(CHUNKS):
-        at = slice(c * step, (c + 1) * step)
-        loads[c][0].wait()
-        loads[c][1].wait()
-        gout += lax.dot_general(grads[:, at], outp[:, at], NT, preferred_element_type=jnp.float32)
-        loads[c][2].wait()
-        loads[c][3].wait()
-        xin += lax.dot_general(acts[:, at], inp[:, at], NT, preferred_element_type=jnp.float32)
+    weight = kept / counted
 
     smalls[1].wait()
     smalls[2].wait()
-    uv[:, 0:rank] = lax.dot_general(
-        gout, outf[...], NT, precision=HIGH, preferred_element_type=jnp.float32
-    )
-    uv[:, rank : 2 * rank] = jnp.dot(
-        xin, inf[...], precision=HIGH, preferred_element_type=jnp.float32
-    )
-    for t in range(used):
-        at = slice(t * queries, (t + 1) * queries)
-        both = uv[pl.ds(t, queries, stride=slots), :] * weight[at]
-        high = both.astype(jnp.bfloat16)
-        low = (both - high.astype(jnp.float32)).astype(jnp.bfloat16)
-        held[me, at, 0 : 2 * rank] = high
-        held[me, at, 2 * rank : 4 * rank] = low
-
-    pl.semaphore_wait(barrier, n - 1 + m - 1)
-
-    def exchange(k):
+
+    def exchange(i, k):
         return pltpu.make_async_remote_copy(
-            src_ref=held.at[me],
-            dst_ref=held.at[me],
-            send_sem=send_sem.at[k],
-            recv_sem=recv_sem.at[k],
+            src_ref=held.at[me, i],
+            dst_ref=held.at[me, i],
+            send_sem=send_sem.at[i, k],
+            recv_sem=recv_sem.at[i, k],
             device_id={"train": lax.rem(me + k, n)},
             device_id_type=MESH,
         )
 
-    def send(k, carry):
-        exchange(k).start()
-        return carry
-
-    lax.fori_loop(1, n, send, 0, unroll=n <= 4)
+    for i, (left, right) in enumerate(((grads, outp), (acts, inp))):
+        total = jnp.zeros((slots * queries, rank), jnp.float32)
+        for c in range(CHUNKS):
+            at = slice(c * step, (c + 1) * step)
+            loads[i][c][0].wait()
+            loads[i][c][1].wait()
+            total += lax.dot_general(
+                left[:, at], right[:, at], NT, preferred_element_type=jnp.float32
+            )
+        factor = outf[...].T if i == 0 else inf[...]
+        total = jnp.dot(total, factor, precision=HIGH, preferred_element_type=jnp.float32)
+        uv[:, 0:rank] = total
+        uv[:, rank : 2 * rank] = total
+        lane = lax.broadcasted_iota(jnp.int32, (queries, 2 * rank), 1)
+        for t in range(used):
+            at = slice(t * queries, (t + 1) * queries)
+            both = uv[pl.ds(t, queries, stride=slots), :]
+            if i == 0:
+                both = both * weight[at]
+            high = both.astype(jnp.bfloat16).astype(jnp.float32)
+            held[me, i, at, :] = jnp.where(lane < rank, high, both - high).astype(jnp.bfloat16)
+        if i == 0:
+            pl.semaphore_wait(barrier, n - 1 + m - 1)
+
+        def send(k, carry):
+            exchange(i, k).start()
+            return carry
+
+        lax.fori_loop(1, n, send, 0, unroll=n <= 4)
 
     def expand(s):
-        block = held[s]
+        block = held[s, 0]
         v = jnp.dot(
-            block, spread[:, wide : wide + 2 * rank], preferred_element_type=jnp.float32
+            held[s, 1], spread[:, wide : wide + 2 * rank], preferred_element_type=jnp.float32
         )
         v = jnp.concatenate([v, v], axis=1)
         for j in range(wide // (4 * rank)):
@@ -181,7 +184,8 @@
     expand(me)
 
     def arrive(k, carry):
-        pltpu.make_async_copy(held.at[me], held.at[me], recv_sem.at[k]).wait()
+        exchange(0, k).wait_recv()
+        exchange(1, k).wait_recv()
         expand(lax.rem(me - k + n, n))
         return carry
 
@@ -195,7 +199,13 @@
         product = lax.dot_general(store[...], pre[b], NT, preferred_element_type=jnp.float32)
         product = jnp.where(valid, product, 0.0)
         for j in range(m):
-            part[j, b] = product[j * share : (j + 1) * share]
+            part[j, b] = jnp.concatenate(
+                [
+                    product[j * share : j * share + share // 2],
+                    product[j * share + share // 2 : (j + 1) * share],
+                ],
+                axis=1,
+            )
         return carry
 
     blocks = n // group
@@ -216,7 +226,8 @@
         reduce(k).start()
 
     def sent(k, carry):
-        exchange(k).wait_send()
+        exchange(0, k).wait_send()
+        exchange(1, k).wait_send()
         return carry
 
     lax.fori_loop(1, n, sent, 0, unroll=n <= 4)
@@ -228,6 +239,7 @@
         for k in range(1, m):
             total += parts_in[k, b]
         size = group * queries
+        total = jnp.concatenate([total[:, 0:size], total[:, size : 2 * size]], axis=0)
         out_ref[pl.ds(pl.multiple_of(b * size, size), size), :] = total.T
         return carry
 
@@ -265,22 +277,22 @@
         pltpu.VMEM((rank, rank), f32),
         pltpu.VMEM((rank, rank), f32),
         pltpu.VMEM((count, wide), bf16),
-        pltpu.VMEM((4 * rank, wide + 2 * rank), bf16),
+        pltpu.VMEM((2 * rank, wide + 2 * rank), bf16),
         pltpu.VMEM((queries * slots, 2 * rank), f32),
-        pltpu.VMEM((n, (slots - 1) * queries, 4 * rank), bf16),
+        pltpu.VMEM((n, 2, (slots - 1) * queries, 2 * rank), bf16),
         pltpu.VMEM((blocks, group * queries, wide), bf16),
-        pltpu.VMEM((m, blocks, share, group * queries), f32),
-        pltpu.VMEM((m, blocks, share, group * queries), f32),
-        pltpu.SemaphoreType.DMA((CHUNKS, 4)),
+        pltpu.VMEM((m, blocks, share // 2, 2 * group * queries), f32),
+        pltpu.VMEM((m, blocks, share // 2, 2 * group * queries), f32),
+        pltpu.SemaphoreType.DMA((2, CHUNKS, 2)),
         pltpu.SemaphoreType.DMA((4,)),
-        pltpu.SemaphoreType.DMA((n,)),
-        pltpu.SemaphoreType.DMA((n,)),
+        pltpu.SemaphoreType.DMA((2, n)),
+        pltpu.SemaphoreType.DMA((2, n)),
         pltpu.SemaphoreType.DMA((m,)),
         pltpu.SemaphoreType.DMA((m,)),
     ]
     return pl.pallas_call(
         functools.partial(kernel, n, m),
-        out_shape=jax.ShapeDtypeStruct((n * queries, share), f32),
+        out_shape=pltpu.VMEM((n * queries, share), f32),
         in_specs=[pl.BlockSpec(memory_space=pl.ANY)] * 8 + [pl.BlockSpec(memory_space=pltpu.SMEM)],
         out_specs=pl.BlockSpec(memory_space=pltpu.VMEM),
         scratch_shapes=scratch,

time: 21.3 us -> 19.5 us (0.915)
  Pallas kernels: 19.1 us -> 18 us
  local copies, waits for them, and re-layouts: 1.38 us -> 0.62 us
    pallas_call x1, Pallas kernels: 19.1 us -> 18 us  [on_device(): pl.pallas_call(functools.partial(kernel, n, m), out_shape=pltpu.VMEM((n *...]
    unnamed x1, local copies, waits for them, and re-layouts: 1.38 us -> 0.62 us
where the time goes in v2:
time: 19.5 us; the launch traced here: 19.3 us
  Pallas kernels  18 us (92%)
  between operations  0.66 us (3%)
  local copies, waits for them, and re-layouts  0.62 us (3%)
    pallas_call x1, Pallas kernels, on_device(): pl.pallas_call(functools.partial(kernel, n, m), out_shape=pltpu.VMEM((n *...  18 us
    unnamed x1, local copies, waits for them, and re-layouts  0.62 us

profile of v2, /device:TPU:0, one launch (start us, length us, event | category | flops | bytes accessed | tf_op | source)
XLA Modules:
  0.0 19.3 jit_solution(9505251730891574712)
XLA Ops:
  0.7 18.0 %shard_map.91 = f32[64,64]{1,0:T(8,128)S(1)} custom-call(s32[8,16]{1,0:T(8,128)} %bitcast.19, bf16[128,5120]{1,0:T(8,128)(2,1)} %bitcast.13, bf16[128,5120]{1,0:T(8,128)(2,1)} %bitcast.14, bf16[64,5120]{1,0:T(8,128)(2,1)} %bitcast.15, bf16[64,5120]{1,0:T(8,128)(2,1)} %bitcast.16, f32[64,64]{1,0:T(8,128)} %bitcast.17, f32[64,64]{1,0:T(8,128)} %bitcast.18, ...), custom_call_target="tpu_custom_call" | custom-call | tf_op jit(solution)/shard_map/pallas_call | solution.py:293
  18.7 0.6 %copy.11 = f32[64,64]{1,0:T(8,128)} copy(f32[64,64]{1,0:T(8,128)S(1)} %shard_map.91) | data formatting | bytes 32768

commit v3 on v2

--- a/solution.py
+++ b/solution.py
@@ -11,7 +11,7 @@
 MESH = pl.DeviceIdType.MESH
 HIGH = lax.Precision.HIGHEST
 NT = (((1,), (1,)), ((), ()))
-CHUNKS = 4
+CHUNKS = 1
 
 
 def onehot(condition):
@@ -101,13 +101,6 @@
     copy.start()
     smalls.append(copy)
 
-    k_at = lax.broadcasted_iota(jnp.int32, (2 * rank, wide), 0) % rank
-    n_at = lax.broadcasted_iota(jnp.int32, (2 * rank, wide), 1) // rank
-    spread[:, 0:wide] = onehot(k_at == n_at)
-    k_at = lax.broadcasted_iota(jnp.int32, (2 * rank, 2 * rank), 0) % rank
-    n_at = lax.broadcasted_iota(jnp.int32, (2 * rank, 2 * rank), 1) % rank
-    spread[:, wide : wide + 2 * rank] = onehot(k_at == n_at)
-
     smalls[0].wait()
     keep = onehot(tok[...] > 0)
     r_at = lax.broadcasted_iota(jnp.int32, (slots * queries, queries), 0)
@@ -163,6 +156,13 @@
             return carry
 
         lax.fori_loop(1, n, send, 0, unroll=n <= 4)
+
+    k_at = lax.broadcasted_iota(jnp.int32, (2 * rank, wide), 0) % rank
+    n_at = lax.broadcasted_iota(jnp.int32, (2 * rank, wide), 1) // rank
+    spread[:, 0:wide] = onehot(k_at == n_at)
+    k_at = lax.broadcasted_iota(jnp.int32, (2 * rank, 2 * rank), 0) % rank
+    n_at = lax.broadcasted_iota(jnp.int32, (2 * rank, 2 * rank), 1) % rank
+    spread[:, wide : wide + 2 * rank] = onehot(k_at == n_at)
 
     def expand(s):
         block = held[s, 0]

time: 19.5 us -> 19 us (0.974)
  Pallas kernels: 18 us -> 17.5 us
    pallas_call x1, Pallas kernels: 18 us -> 17.5 us  [on_device(): pl.pallas_call(functools.partial(kernel, n, m), out_shape=pltpu.VMEM((n *...]
where the time goes in v3:
time: 19 us; the launch traced here: 18.8 us
  Pallas kernels  17.5 us (92%)
  between operations  0.66 us (3%)
  local copies, waits for them, and re-layouts  0.62 us (3%)
    pallas_call x1, Pallas kernels, on_device(): pl.pallas_call(functools.partial(kernel, n, m), out_shape=pltpu.VMEM((n *...  17.5 us
    unnamed x1, local copies, waits for them, and re-layouts  0.62 us

profile of v3, /device:TPU:0, one launch (start us, length us, event | category | flops | bytes accessed | tf_op | source)
XLA Modules:
  0.0 18.8 jit_solution(2428050196142061918)
XLA Ops:
  0.7 17.5 %shard_map.91 = f32[64,64]{1,0:T(8,128)S(1)} custom-call(s32[8,16]{1,0:T(8,128)} %bitcast.19, bf16[128,5120]{1,0:T(8,128)(2,1)} %bitcast.13, bf16[128,5120]{1,0:T(8,128)(2,1)} %bitcast.14, bf16[64,5120]{1,0:T(8,128)(2,1)} %bitcast.15, bf16[64,5120]{1,0:T(8,128)(2,1)} %bitcast.16, f32[64,64]{1,0:T(8,128)} %bitcast.17, f32[64,64]{1,0:T(8,128)} %bitcast.18, ...), custom_call_target="tpu_custom_call" | custom-call | tf_op jit(solution)/shard_map/pallas_call | solution.py:293
  18.2 0.6 %copy.11 = f32[64,64]{1,0:T(8,128)} copy(f32[64,64]{1,0:T(8,128)S(1)} %shard_map.91) | data formatting | bytes 32768

commit v4 on v3

--- a/solution.py
+++ b/solution.py
@@ -189,7 +189,7 @@
         expand(lax.rem(me - k + n, n))
         return carry
 
-    lax.fori_loop(1, n, arrive, 0)
+    lax.fori_loop(1, n, arrive, 0, unroll=n <= 4)
 
     smalls[3].wait()
     r_at = lax.broadcasted_iota(jnp.int32, (store.shape[0], 1), 0)

time: 19 us -> 19 us (level)
  no operation moved by 1% of the time
where the time goes in v4:
time: 19 us; the launch traced here: 18.8 us
  Pallas kernels  17.5 us (92%)
  between operations  0.66 us (3%)
  local copies, waits for them, and re-layouts  0.62 us (3%)
    pallas_call x1, Pallas kernels, on_device(): pl.pallas_call(functools.partial(kernel, n, m), out_shape=pltpu.VMEM((n *...  17.5 us
    unnamed x1, local copies, waits for them, and re-layouts  0.62 us

profile of v4, /device:TPU:0, one launch (start us, length us, event | category | flops | bytes accessed | tf_op | source)
XLA Modules:
  0.0 18.8 jit_solution(13762467038902605976)
XLA Ops:
  0.7 17.5 %shard_map.91 = f32[64,64]{1,0:T(8,128)S(1)} custom-call(s32[8,16]{1,0:T(8,128)} %bitcast.19, bf16[128,5120]{1,0:T(8,128)(2,1)} %bitcast.13, bf16[128,5120]{1,0:T(8,128)(2,1)} %bitcast.14, bf16[64,5120]{1,0:T(8,128)(2,1)} %bitcast.15, bf16[64,5120]{1,0:T(8,128)(2,1)} %bitcast.16, f32[64,64]{1,0:T(8,128)} %bitcast.17, f32[64,64]{1,0:T(8,128)} %bitcast.18, ...), custom_call_target="tpu_custom_call" | custom-call | tf_op jit(solution)/shard_map/pallas_call | solution.py:293
  18.2 0.6 %copy.11 = f32[64,64]{1,0:T(8,128)} copy(f32[64,64]{1,0:T(8,128)S(1)} %shard_map.91) | data formatting | bytes 32768
